TPU v7x, 256 devices: a whole 4x4x8 slice. The times are simulated.
256 devices in a mesh: samples: 128 (over x_hi, y, z, core), feat: 2 (over x_lo).
Axes of the slice: x: 4 (x_hi: 2, x_lo: 2; x = x_hi * 2 + x_lo), y: 4, z: 8, core: 2. Of those that a mesh axis runs over, the one named last changes fastest.
Arguments:
- samples: float32 [32768, 4096], P('samples', 'feat'), may hold values from -12 to 12, as said below
- factor: float32 [4096, 512], P('feat'), may hold values from -6 to 6
Outputs:
- new_factor: float32 [4096, 512], P('feat')
Inputs may be any that keep to these rules, and one draw needn't show every extreme that they name: `samples`: Real-valued data.
All inputs are finite; a program needn't handle non-finite values.
Results may differ from a plain program's by a relative error of at most 0.00007.
Values sent between devices are 32-bit elements; how exact they have to be, the bound alone decides.
A program may use at most 64 MiB of HBM per device.

v0:
```python
import jax
import jax.numpy as jnp
from jax import lax
from jax.sharding import PartitionSpec as P

D = 4096
R = 512


def per_device(samples, factor):
    high = lax.Precision.HIGHEST
    contract_rows = (((0,), (0,)), ((), ()))
    scaled = factor * (1.0 / jnp.sqrt(jnp.float32(D)))
    local_proj = jnp.dot(samples, scaled, precision=high, preferred_element_type=jnp.float32)
    proj = lax.psum(local_proj, "feat")
    squared = proj * proj
    rows_total = samples.shape[0] * lax.axis_size("samples")
    owned = factor.shape[0] // lax.axis_size("samples")
    owned_start = lax.axis_index("samples") * owned
    owned_scaled = lax.dynamic_slice_in_dim(scaled, owned_start, owned, 0)
    half_gram = lax.dot_general(
        scaled, scaled, contract_rows, precision=high, preferred_element_type=jnp.float32
    )
    gram = lax.psum(half_gram, "feat")
    squared_gram = gram * gram
    coef = 6.0 / jnp.sqrt(jnp.float32(D))
    moment = (
        lax.psum_scatter(
            lax.dot_general(
                samples, squared, contract_rows, precision=high, preferred_element_type=jnp.float32
            ),
            "samples",
            scatter_dimension=0,
            tiled=True,
        )
        / rows_total
    )
    gram_term = jnp.dot(
        owned_scaled, squared_gram, precision=high, preferred_element_type=jnp.float32
    )
    grad = coef * (gram_term - moment)
    total = lax.psum(jnp.sum(grad * grad), ("samples", "feat"))
    rms = jnp.sqrt(total / (D * R)) + 1e-06
    owned_factor = lax.dynamic_slice_in_dim(factor, owned_start, owned, 0)
    updated = owned_factor - 0.5 * grad / rms
    return lax.all_gather(updated, "samples", axis=0, tiled=True)


def solution(mesh):
    placed = (P("samples", "feat"), P("feat", None))
    return jax.shard_map(
        per_device, mesh=mesh, in_specs=placed, out_specs=P("feat", None), check_vma=False
    )
```

profile of v0, /device:TPU:1, one launch (start us, length us, event | category | flops | bytes accessed | tf_op | source)
XLA Modules:
  0.0 967.5 jit_solution(6037234645448429249)
XLA Ops:
  6.5 0.0 copy-start
  6.5 0.0 all-reduce.3.cloned.1.call-start
  6.5 0.0 copy-start.1
  6.5 11.3 %fusion.4 = f32[512,512]{1,0:T(8,128)} fusion(f32[2048,512]{1,0:T(8,128)} %param.3), kind=kOutput, calls=%fused_computation.10 | convolution fusion | flops 6443499520 | bytes 5242880 | tf_op jit(solution)/shard_map/dot_general | solution.py:21
  17.8 0.0 copy-done
  17.8 0.0 copy-done.1
  17.9 7.5 convolution_bitcast_fusion.1
  25.4 0.0 all-reduce.3.cloned.1.call-update
  25.4 0.2 reduce-scatter.2.cloned.1.call-start
  25.6 67.1 %all-reduce.3.cloned.1.call-done = (f32[512,512]{1,0:T(8,128)}, f32[256,512]{0,1:T(8,128)}) async-done(((f32[512,512]{1,0:T(8,128)}, f32[256,512]{0,1:T(8,128)}), (f32[512,512]{1,0:T(8,128)}, f32[256,512]{0,1:T(8,128)})) %all-reduce.3.cloned.1.call-update) | async-done | bytes 1572880 | tf_op jit(solution)/shard_map/psum | solution.py:24
  92.7 6.1 convolution_bitcast_fusion
  98.9 0.0 reduce-scatter.2.cloned.1.call-update
  98.9 0.0 all-gather.2.cloned.1.call-start
  99.0 0.0 copy-start.2
  99.0 4.7 broadcast_multiply_fusion
  103.7 654.4 %reduce-scatter.2.cloned.1.call-done = f32[16,512]{1,0:T(8,128)} async-done(((f32[2048,512]{1,0:T(8,128)}), f32[16,512]{1,0:T(8,128)}) %reduce-scatter.2.cloned.1.call-update) | async-done | bytes 32784 | tf_op jit(solution)/shard_map/reduce_scatter | solution.py:28
  758.1 0.0 copy-done.2
  758.1 2.0 multiply_reduce_fusion
  760.1 79.2 %psum.23 = f32[]{:T(128)} all-reduce(f32[]{:T(128)} %get-tuple-element.7), channel_id=1, replica_groups=mesh['samples'=128,'feat'=2] {'samples','feat'}, use_global_device_ids=true, to_apply=%region_4.0 | all-reduce | flops 1 | bytes 8 | tf_op jit(solution)/shard_map/psum | solution.py:42
  840.0 1.4 divide_subtract_fusion
  841.4 0.0 all-gather.2.cloned.1.call-update
  841.4 114.9 %all-gather.2.cloned.1.call-done = f32[2048,512]{1,0:T(8,128)} async-done(((f32[16,512]{1,0:T(8,128)}), f32[2048,512]{1,0:T(8,128)}) %all-gather.2.cloned.1.call-update) | async-done | bytes 4194320 | tf_op jit(solution)/shard_map/all_gather | solution.py:46
  956.3 4.6 copy.8
Async XLA Ops:
  6.5 11.3 %copy-start = (f32[256,2048]{1,0:T(8,128)S(1)}, f32[256,2048]{1,0:T(8,128)}, u32[]{:S(2)}) copy-start(f32[256,2048]{1,0:T(8,128)} %param.2) | copy-start | bytes 6291460
  6.5 86.2 %all-reduce.3.cloned.1.call-start = ((), (), s32[]{:S(2)}) async-start(), calls=%async_computation.3 | async-start | bytes 3145728 | tf_op jit(solution)/shard_map/psum | solution.py:24
  6.5 11.3 %copy-start.1 = (f32[2048,512]{1,0:T(8,128)S(1)}, f32[2048,512]{1,0:T(8,128)}, u32[]{:S(2)}) copy-start(f32[2048,512]{1,0:T(8,128)} %param.3) | copy-start | bytes 12582916
  25.4 732.7 %reduce-scatter.2.cloned.1.call-start = ((), (), s32[]{:S(2)}) async-start(), calls=%async_computation.1 | async-start | bytes 4227072 | tf_op jit(solution)/shard_map/reduce_scatter | solution.py:28
  98.9 857.4 %all-gather.2.cloned.1.call-start = ((), (), s32[]{:S(2)}) async-start(), calls=%async_computation.2 | async-start | bytes 4227072 | tf_op jit(solution)/shard_map/all_gather | solution.py:46
  99.0 659.1 %copy-start.2 = (f32[512,512]{1,0:T(8,128)S(1)}, f32[512,512]{1,0:T(8,128)}, u32[]{:S(2)}) copy-start(f32[512,512]{1,0:T(8,128)} %get-tuple-element.5) | copy-start | bytes 3145732
Sparse Core Ops, SparseCore 0:
  25.5 67.1 all-reduce.2
  99.0 659.0 reduce-scatter.1
  841.5 114.7 all-gather.1
where the time goes:
time: 968 us; the launch traced here: 967 us
  waiting for transfers between devices  836 us (86%)
  blocking collectives  79.2 us (8%)
  matrix products  27 us (3%)
  between operations  13.8 us (1%)
    reduce_scatter x1, waiting for transfers between devices, per_device(): lax.psum_scatter(lax.dot_general(samples, squared, contract_rows, precisi...  654 us
    all_gather x1, waiting for transfers between devices, per_device(): return lax.all_gather(updated, 'samples', axis=0, tiled=True)  115 us
    psum x1, blocking collectives, per_device(): total = lax.psum(jnp.sum(grad * grad), ('samples', 'feat'))  79.2 us
    psum x1, waiting for transfers between devices, per_device(): gram = lax.psum(half_gram, 'feat')  67.1 us
  transfers between devices with their start and end apart: 3, of which 3 were waited for; matrix products, arithmetic and copies ran while one was open for 0% of the time, Pallas kernels for 0%

commit v1 on v0

v1 whole, which is shorter than its diff:
```python
import jax
import jax.numpy as jnp
from jax import lax
from jax.experimental import pallas as pl
from jax.experimental.pallas import tpu as pltpu
from jax.sharding import PartitionSpec as P

D = 4096
R = 512
NROWS = 32768
HALF = D // 2
ROWS = 256
COLS = 256
MINE = HALF // 2
MESH = pl.DeviceIdType.MESH
F32 = jnp.float32
BF16 = jnp.bfloat16

STREAMS = ((1, 0, 4), (-1, 1, 4), (1, 1, 3), (-1, 0, 3))
SLOT = {}
for _k in range(1, 5):
    for _i, (_, _, _hops) in enumerate(STREAMS):
        if _k <= _hops:
            SLOT[(_i, _k)] = len(SLOT)
NSLOT = len(SLOT)


def split(v):
    hi = v.astype(BF16)
    return hi, (v - hi.astype(F32)).astype(BF16)


def dot3(ah, al, bh, bl, dims=(((1,), (0,)), ((), ()))):
    def one(a, b):
        return lax.dot_general(a, b, dims, preferred_element_type=F32)

    return one(ah, bh) + (one(ah, bl) + one(al, bh))


def kernel(
    x_hbm, f_hbm, o_ref,
    xv, xo, fv, fh, fl, xh, xl, p, pr, s, so, xth, xtl, mom,
    ring, acc_a, dir_a, yrecv, acc_b, zrecv, acc_b2, xrecv,
    g, gr, g2, grad_a, grad_b, ss1, ss2, ss3, ss4,
    load_sem, send, recv,
):
    sidx = lax.axis_index("samples")
    feat = lax.axis_index("feat")
    core = lax.rem(sidx, 2)
    z = lax.rem(sidx // 2, 8)
    y = lax.rem(sidx // 16, 4)
    xhi = sidx // 64

    def dev(a, b, c, d, e):
        return (((a * 4 + b) * 8 + c) * 2 + d, e)

    other = dev(xhi, y, z, 1 - core, feat)
    partner = dev(xhi, y, z, core, 1 - feat)

    def yx_of(j):
        return lax.rem(y + j // 2, 4), lax.rem(xhi + j % 2, 2)

    def yx_peer(j):
        a, b = yx_of(j)
        return dev(b, a, z, core, feat)

    def z_of(j):
        return lax.rem(z + j + 8, 8)

    def z_peer(j):
        return dev(xhi, y, z_of(j), core, feat)

    counter = [0]

    def start(src, dst, to):
        i = counter[0]
        counter[0] += 1
        c = pltpu.make_async_remote_copy(
            src_ref=src, dst_ref=dst, send_sem=send.at[i], recv_sem=recv.at[i],
            device_id=to, device_id_type=MESH,
        )
        c.start()
        return c

    loads = []
    for i in range(2):
        loads.append(pltpu.make_async_copy(f_hbm.at[:, pl.ds(i * COLS, COLS)], fv.at[i], load_sem.at[i]))
    loads.append(pltpu.make_async_copy(x_hbm, xv, load_sem.at[2]))
    loads[2].start()
    loads[0].start()
    loads[1].start()
    barrier = pltpu.get_barrier_semaphore()
    everyone = [other, partner] + [yx_peer(j) for j in range(1, 8)] + [z_peer(j) for j in range(1, 8)]
    for to in everyone:
        pl.semaphore_signal(barrier, inc=1, device_id=to, device_id_type=MESH)
    loads[2].wait()

    def split_x(i, _):
        r = pl.ds(i * 32, 32)
        xh[r, :], xl[r, :] = split(xv[r, :])
        return 0

    lax.fori_loop(0, ROWS // 32, split_x, 0)

    def split_f(h):
        def body(i, _):
            r = pl.ds(pl.multiple_of(i * 128, 128), 128)
            fh[h, r, :], fl[h, r, :] = split(fv[h, r, :])
            return 0

        lax.fori_loop(0, HALF // 128, body, 0)

    def project(h):
        p[h] = jnp.zeros((ROWS, COLS), F32)

        def body(k, _):
            r = pl.ds(pl.multiple_of(k * 512, 512), 512)
            p[h] += dot3(xh[:, r], xl[:, r], fh[h, r, :], fl[h, r, :])
            return 0

        lax.fori_loop(0, HALF // 512, body, 0)


    loads[0].wait()
    split_f(0)
    project(0)
    pl.semaphore_wait(barrier, len(everyone))
    proj_copy = [start(p.at[0], pr.at[0], partner)]
    x_copy = start(x_hbm.at[:, pl.ds(pl.multiple_of((1 - core) * MINE, MINE), MINE)], xo, other)
    loads[1].wait()
    split_f(1)
    project(1)
    proj_copy.append(start(p.at[1], pr.at[1], partner))

    def turn(src, base, at):
        def body(i, _):
            c = pl.ds(pl.multiple_of(base + i * 128, 128), 128)
            r = pl.ds(pl.multiple_of(i * 128, 128), 128)
            hi, lo = split(src[:, c].T)
            xth[r, at : at + ROWS] = hi
            xtl[r, at : at + ROWS] = lo
            return 0

        lax.fori_loop(0, MINE // 128, body, 0)

    turn(xv, core * MINE, 0)
    x_copy.wait()
    turn(xo, 0, ROWS)

    contract = (((0,), (0,)), ((), ()))
    g[...] = jnp.zeros_like(g)

    def gram_body(k, _):
        r = pl.ds(pl.multiple_of(k * 512, 512), 512)
        ah, al = fh[core, r, :], fl[core, r, :]
        for h in range(2):
            g[:, h * COLS : (h + 1) * COLS] += dot3(ah, al, fh[h, r, :], fl[h, r, :], contract)
        return 0

    lax.fori_loop(0, HALF // 512, gram_body, 0)

    s_copy = []
    for h in range(2):
        proj_copy[h].wait()
        total = p[h] + pr[h]
        s[h] = total * total
        s_copy.append(start(s.at[h], so.at[h], other))
    g_copy = start(g, gr, partner)

    def moment(h):
        ah, al = split(s[h])
        bh, bl = split(so[h])
        sh = jnp.concatenate([ah, bh], axis=0)
        sl = jnp.concatenate([al, bl], axis=0)

        def body(i, _):
            r = pl.ds(pl.multiple_of(i * 256, 256), 256)
            mom[h, r, :] = dot3(xth[r, :], xtl[r, :], sh, sl)
            return 0

        lax.fori_loop(0, MINE // 256, body, 0)

    def zrows(zz, half):
        return pl.ds(pl.multiple_of(zz * 128 + half * 64, 64), 64)

    ring_copy = {}

    def ring_step(k):
        for i, (way, half, hops) in enumerate(STREAMS):
            if k > hops:
                continue
            r = zrows(z_of(way * (hops + 1 - k)), half)
            if k > 1:
                ring_copy[(i, k - 1)].wait_recv()
                mom[0, r, :] += ring[SLOT[(i, k - 1)]]
            ring_copy[(i, k)] = start(mom.at[0, r, :], ring.at[SLOT[(i, k)]], z_peer(way))

    s_copy[0].wait()
    moment(0)
    ring_step(1)
    s_copy[1].wait()
    moment(1)
    y_copy = {}
    for j in (2, 1, 3):
        yy = lax.rem(y + j, 4)
        y_copy[j] = start(
            mom.at[1, pl.ds(pl.multiple_of(yy * 256, 256), 256), :], yrecv.at[j - 1], dev(xhi, yy, z, core, feat)
        )
    ring_step(2)

    g_copy.wait()
    whole = (g[...] + gr[...]) * (1.0 / D)
    g2[core] = whole * whole
    g2_copy = start(g2.at[core], g2.at[core], other)

    ring_step(3)
    ring_step(4)

    for half in range(2):
        parts = []
        for i, (way, h, hops) in enumerate(STREAMS):
            if h == half:
                ring_copy[(i, hops)].wait_recv()
                parts.append(ring[SLOT[(i, hops)]])
        acc_a[half * 64 : half * 64 + 64, :] = mom[0, zrows(z, half), :] + (parts[0] + parts[1])
    da_copy = {}
    for j in range(1, 8):
        a, b = yx_of(j)
        r = pl.ds(pl.multiple_of(a * 32 + b * 16, 16), 16)
        da_copy[j] = start(acc_a.at[r, :], dir_a.at[j - 1], yx_peer(j))

    for j in (1, 3, 2):
        y_copy[j].wait_recv()
    acc_b[...] = (mom[1, pl.ds(pl.multiple_of(y * 256, 256), 256), :] + yrecv[0]) + (yrecv[1] + yrecv[2])
    zb_copy = {}
    for j in (4, 3, 5, 2, 6, 1, 7):
        r = pl.ds(pl.multiple_of(z_of(j) * 32, 32), 32)
        zb_copy[j] = start(acc_b.at[r, :], zrecv.at[j - 1], z_peer(j))

    g2_copy.wait()
    scale = 6.0 / 64.0

    def finish(h, at, total):
        at = pl.multiple_of(at, 16)
        term = jnp.zeros((16, COLS), F32)
        for q in range(2):
            ah, al = split(fv[q, pl.ds(at, 16), :] * (1.0 / 64.0))
            bh, bl = split(g2[q, :, h * COLS : (h + 1) * COLS])
            term += dot3(ah, al, bh, bl)
        return scale * (term - total * (1.0 / (NROWS * D)))

    row_a = core * MINE + z * 128 + y * 32 + xhi * 16
    row_b = core * MINE + y * 256 + z * 32 + xhi * 16
    own_a = acc_a[pl.ds(pl.multiple_of(y * 32 + xhi * 16, 16), 16), :]
    for j in range(1, 8):
        da_copy[j].wait_recv()
    for j in range(1, 8):
        own_a = own_a + dir_a[j - 1]
    ga = finish(0, row_a, own_a)
    mine_a = pl.ds(pl.multiple_of(row_a, 16), 16)
    grad_a[mine_a, :] = ga
    aa_copy = {}
    for j in range(1, 8):
        aa_copy[j] = start(grad_a.at[mine_a, :], grad_a.at[mine_a, :], yx_peer(j))

    for j in range(1, 8):
        zb_copy[j].wait_recv()
    own_b = acc_b[pl.ds(pl.multiple_of(z * 32, 32), 32), :]
    for j in range(1, 8):
        own_b = own_b + zrecv[j - 1]
    acc_b2[...] = own_b
    xb_copy = start(acc_b2.at[pl.ds(pl.multiple_of((1 - xhi) * 16, 16), 16), :], xrecv, yx_peer(1))

    for j in range(1, 8):
        aa_copy[j].wait_recv()
    base = core * MINE
    gather = {}
    forward = []

    def grows(zz, half):
        return pl.ds(pl.multiple_of(base + zz * 128 + half * 64, 64), 64)

    def gather_step(k):
        for i, (way, half, hops) in enumerate(STREAMS):
            if k > hops:
                continue
            r = grows(z_of(-way * (k - 1)), half)
            if k > 1:
                gather[(i, k - 1)].wait_recv()
            gather[(i, k)] = start(grad_a.at[r, :], grad_a.at[r, :], z_peer(way))
            if k > 1:
                forward.append(start(grad_a.at[r, :], grad_a.at[r, :], other))

    gather_step(1)
    r = pl.ds(pl.multiple_of(base + z * 128, 128), 128)
    forward.append(start(grad_a.at[r, :], grad_a.at[r, :], other))

    xb_copy.wait_recv()
    gb = finish(1, row_b, acc_b2[pl.ds(pl.multiple_of(xhi * 16, 16), 16), :] + xrecv[...])
    mine_b = pl.ds(pl.multiple_of(row_b, 16), 16)
    grad_b[mine_b, :] = gb
    xg_copy = start(grad_b.at[mine_b, :], grad_b.at[mine_b, :], yx_peer(1))

    sq = ga * ga + gb * gb
    tile = (sq[0:8, 0:128] + sq[8:16, 0:128]) + (sq[0:8, 128:256] + sq[8:16, 128:256])
    me1 = y * 2 + xhi
    ss1[me1] = tile
    s1_copy = [start(ss1.at[me1], ss1.at[me1], yx_peer(j)) for j in range(1, 8)]

    gather_step(2)
    xg_copy.wait_recv()
    pair = pl.ds(pl.multiple_of(base + y * 256 + z * 32, 32), 32)
    zg_copy = [start(grad_b.at[pair, :], grad_b.at[pair, :], z_peer(j)) for j in (4, 3, 5, 2, 6, 1, 7)]
    for c in s1_copy:
        c.wait_recv()
    tile = ss1[0]
    for j in range(1, 8):
        tile = tile + ss1[j]
    ss2[z] = tile
    s2_copy = [start(ss2.at[z], ss2.at[z], z_peer(j)) for j in range(1, 8)]
    gather_step(3)
    for c in zg_copy:
        c.wait_recv()
    block = pl.ds(pl.multiple_of(base + y * 256, 256), 256)
    yg_copy = {}
    for j in (2, 1, 3):
        yy = lax.rem(y + j, 4)
        yg_copy[j] = start(grad_b.at[block, :], grad_b.at[block, :], dev(xhi, yy, z, core, feat))
    forward.append(start(grad_b.at[block, :], grad_b.at[block, :], other))
    for c in s2_copy:
        c.wait_recv()
    tile = ss2[0]
    for j in range(1, 8):
        tile = tile + ss2[j]
    ss3[core] = tile
    s3_copy = start(ss3.at[core], ss3.at[core], other)
    gather_step(4)
    s3_copy.wait_recv()
    ss4[feat] = ss3[0] + ss3[1]
    s4_copy = start(ss4.at[feat], ss4.at[feat], partner)

    for i, (way, half, hops) in enumerate(STREAMS):
        gather[(i, hops)].wait_recv()
        r = grows(z_of(-way * hops), half)
        forward.append(start(grad_a.at[r, :], grad_a.at[r, :], other))
    for j in (1, 3, 2):
        yg_copy[j].wait_recv()
        r = pl.ds(pl.multiple_of(base + lax.rem(y - j + 4, 4) * 256, 256), 256)
        forward.append(start(grad_b.at[r, :], grad_b.at[r, :], other))
    s4_copy.wait_recv()
    total = jnp.sum(ss4[0] + ss4[1], keepdims=True)
    rms = jnp.sqrt(total * (1.0 / (D * R))) + 1e-06
    step = 0.5 / rms
    for c in forward:
        c.wait_recv()

    def update(i, _):
        r = pl.ds(pl.multiple_of(i * 128, 128), 128)
        o_ref[r, 0:COLS] = fv[0, r, :] - grad_a[r, :] * step
        o_ref[r, COLS:R] = fv[1, r, :] - grad_b[r, :] * step
        return 0

    lax.fori_loop(0, HALF // 128, update, 0)

    sends = list(ring_copy.values()) + list(y_copy.values()) + list(da_copy.values()) + list(zb_copy.values())
    sends += list(aa_copy.values()) + [xb_copy] + list(gather.values()) + forward + [xg_copy] + s1_copy + zg_copy
    sends += s2_copy + list(yg_copy.values()) + [s3_copy, s4_copy]
    for c in sends:
        c.wait_send()


NSEM = 160


def per_device(samples, factor):
    vm = pltpu.VMEM
    scratch = [
        vm((ROWS, HALF), F32), vm((ROWS, MINE), F32), vm((2, HALF, COLS), F32),
        vm((2, HALF, COLS), BF16), vm((2, HALF, COLS), BF16),
        vm((ROWS, HALF), BF16), vm((ROWS, HALF), BF16),
        vm((2, ROWS, COLS), F32), vm((2, ROWS, COLS), F32), vm((2, ROWS, COLS), F32), vm((2, ROWS, COLS), F32),
        vm((MINE, 2 * ROWS), BF16), vm((MINE, 2 * ROWS), BF16), vm((2, MINE, COLS), F32),
        vm((NSLOT, 64, COLS), F32), vm((128, COLS), F32), vm((7, 16, COLS), F32),
        vm((3, 256, COLS), F32), vm((256, COLS), F32), vm((7, 32, COLS), F32), vm((32, COLS), F32), vm((16, COLS), F32),
        vm((256, R), F32), vm((256, R), F32), vm((2, 256, R), F32),
        vm((HALF, COLS), F32), vm((HALF, COLS), F32),
        vm((8, 8, 128), F32), vm((8, 8, 128), F32), vm((2, 8, 128), F32), vm((2, 8, 128), F32),
        pltpu.SemaphoreType.DMA((3,)), pltpu.SemaphoreType.DMA((NSEM,)), pltpu.SemaphoreType.DMA((NSEM,)),
    ]
    return pl.pallas_call(
        kernel,
        out_shape=jax.ShapeDtypeStruct((HALF, R), F32),
        in_specs=[pl.BlockSpec(memory_space=pl.ANY)] * 2,
        out_specs=pl.BlockSpec(memory_space=pltpu.VMEM),
        scratch_shapes=scratch,
        name="cp_step",
        cost_estimate=pl.CostEstimate(flops=10**10, bytes_accessed=10**7, transcendentals=0),
        compiler_params=pltpu.CompilerParams(
            collective_id=0, has_side_effects=True, vmem_limit_bytes=50 * 2**20
        ),
    )(samples, factor)


def solution(mesh):
    placed = (P("samples", "feat"), P("feat", None))
    return jax.shard_map(
        per_device, mesh=mesh, in_specs=placed, out_specs=P("feat", None), check_vma=False
    )
```

time: 968 us -> 91.7 us (0.09)
  waiting for transfers between devices: 836 us -> 0 us
  Pallas kernels: 0 us -> 85.3 us
  blocking collectives: 79.2 us -> 0 us
  matrix products: 27 us -> 0 us
  between operations: 13.8 us -> 0.01 us
    reduce_scatter x1 -> x0, waiting for transfers between devices: 654 us -> none  [per_device(): lax.psum_scatter(lax.dot_general(samples, squared, contract_rows, precisi...]
    all_gather x1 -> x0, waiting for transfers between devices: 115 us -> none  [per_device(): return lax.all_gather(updated, 'samples', axis=0, tiled=True)]
    pallas_call x0 -> x1, Pallas kernels: none -> 85.3 us  [per_device(): pl.pallas_call(kernel, out_shape=jax.ShapeDtypeStruct((HALF, R), F32), in...]
    psum x1 -> x0, blocking collectives: 79.2 us -> none  [per_device(): total = lax.psum(jnp.sum(grad * grad), ('samples', 'feat'))]
    psum x1 -> x0, waiting for transfers between devices: 67.1 us -> none  [per_device(): gram = lax.psum(half_gram, 'feat')]
    dot_general x4 -> x0, matrix products: 27 us -> none  [the longest x1 11.3 us: per_device(): lax.dot_general(scaled, scaled, contract_rows, precision=high, preferred_...]
  transfers between devices with their start and end apart: 3 -> 0, of which waited for: 3 -> 0; matrix products, arithmetic and copies ran while one was open for 0% -> 0% of each run, Pallas kernels for 0% -> 0%
where the time goes in v1:
time: 91.7 us; the launch traced here: 91.6 us
  Pallas kernels  85.3 us (93%)
  local copies, waits for them, and re-layouts  6.23 us (7%)
    pallas_call x1, Pallas kernels, per_device(): pl.pallas_call(kernel, out_shape=jax.ShapeDtypeStruct((HALF, R), F32), in...  85.3 us
    unnamed x3, local copies, waits for them, and re-layouts  6.23 us

profile of v1, /device:TPU:1, one launch (start us, length us, event | category | flops | bytes accessed | tf_op | source)
XLA Modules:
  0.0 91.6 jit_solution(8405935546110102749)
XLA Ops:
  0.0 0.0 copy-start
  0.0 1.6 %copy-done = f32[256,2048]{1,0:T(8,128)S(1)} copy-done((f32[256,2048]{1,0:T(8,128)S(1)}, f32[256,2048]{1,0:T(8,128)}, u32[]{:S(2)}) %copy-start) | copy-done | bytes 2097176
  1.6 85.3 %cp_step.1 = f32[2048,512]{1,0:T(8,128)} custom-call(f32[256,2048]{1,0:T(8,128)S(1)} %copy-done, f32[2048,512]{1,0:T(8,128)} %f_hbm.1), custom_call_target="tpu_custom_call" | custom-call | flops 10000000000 | bytes 10000000 | tf_op jit(solution)/shard_map/cp_step/pallas_call | solution.py:390
  86.9 4.6 %copy.4 = f32[2048,512]{1,0:T(8,128)} copy(f32[2048,512]{1,0:T(8,128)} %cp_step.1) | data formatting | bytes 8388608
Async XLA Ops:
  0.0 1.6 %copy-start = (f32[256,2048]{1,0:T(8,128)S(1)}, f32[256,2048]{1,0:T(8,128)}, u32[]{:S(2)}) copy-start(f32[256,2048]{1,0:T(8,128)} %x_hbm.1) | copy-start | bytes 6291460

commit v2 on v1

v2 whole, which is shorter than its diff:
```python
import jax
import jax.numpy as jnp
from jax import lax
from jax.experimental import pallas as pl
from jax.experimental.pallas import tpu as pltpu
from jax.sharding import PartitionSpec as P

D = 4096
R = 512
NROWS = 32768
HALF = D // 2
ROWS = 256
COLS = 256
DEPTH = 512
MINE = HALF // 2
MESH = pl.DeviceIdType.MESH
F32 = jnp.float32
BF16 = jnp.bfloat16

STREAMS = ((1, 0, 4), (-1, 1, 4), (1, 1, 3), (-1, 0, 3))
SLOT = {}
for _k in range(1, 5):
    for _i, (_, _, _hops) in enumerate(STREAMS):
        if _k <= _hops:
            SLOT[(_i, _k)] = len(SLOT)
NSLOT = len(SLOT)


def split(v):
    hi = v.astype(BF16)
    return hi, (v - hi.astype(F32)).astype(BF16)


def dot3(ah, al, bh, bl, dims=(((1,), (0,)), ((), ()))):
    def one(a, b):
        return lax.dot_general(a, b, dims, preferred_element_type=F32)

    return one(ah, bh) + (one(ah, bl) + one(al, bh))


def kernel(
    x_hbm, f_hbm, o_ref,
    xv, xo, fv, fh, fl, xh, xl, p, pr, s, so, xth, xtl, mom,
    ring, acc_a, dir_a, yrecv, acc_b, zrecv, acc_b2, xrecv,
    g, gr, g2, term, grad, ss1, ss2, ss3, ss4,
    load_sem, send, recv,
):
    sidx = lax.axis_index("samples")
    feat = lax.axis_index("feat")
    core = lax.rem(sidx, 2)
    z = lax.rem(sidx // 2, 8)
    y = lax.rem(sidx // 16, 4)
    xhi = sidx // 64

    def dev(a, b, c, d, e):
        return (((a * 4 + b) * 8 + c) * 2 + d, e)

    other = dev(xhi, y, z, 1 - core, feat)
    partner = dev(xhi, y, z, core, 1 - feat)

    def yx_of(j):
        return lax.rem(y + j // 2, 4), lax.rem(xhi + j % 2, 2)

    def yx_peer(j):
        a, b = yx_of(j)
        return dev(b, a, z, core, feat)

    def y_of(j):
        return lax.rem(y + j + 4, 4)

    def y_peer(j):
        return dev(xhi, y_of(j), z, core, feat)

    def z_of(j):
        return lax.rem(z + j + 8, 8)

    def z_peer(j):
        return dev(xhi, y, z_of(j), core, feat)

    def span(at, n):
        return pl.ds(pl.multiple_of(at, 16), n)

    counter = [0]
    unsent = []

    def start(src, dst, to):
        i = counter[0]
        counter[0] += 1
        c = pltpu.make_async_remote_copy(
            src_ref=src, dst_ref=dst, send_sem=send.at[i], recv_sem=recv.at[i],
            device_id=to, device_id_type=MESH,
        )
        c.start()
        unsent.append(c)
        return c

    def kspan(k):
        return pl.ds(k * DEPTH, DEPTH)

    load_x = [pltpu.make_async_copy(x_hbm.at[:, kspan(k)], xv.at[:, kspan(k)], load_sem.at[k]) for k in range(4)]
    load_f = [
        [
            pltpu.make_async_copy(
                f_hbm.at[kspan(k), pl.ds(h * COLS, COLS)], fv.at[h, kspan(k), :], load_sem.at[4 + 4 * h + k]
            )
            for k in range(4)
        ]
        for h in range(2)
    ]
    for k in range(4):
        load_x[k].start()
        load_f[0][k].start()
    for k in range(4):
        load_f[1][k].start()
    barrier = pltpu.get_barrier_semaphore()
    everyone = [other, partner] + [yx_peer(j) for j in range(1, 8)] + [z_peer(j) for j in range(1, 8)]
    for to in everyone:
        pl.semaphore_signal(barrier, inc=1, device_id=to, device_id_type=MESH)

    def project(h):
        for k in range(4):
            if h == 0:
                load_x[k].wait()

                def split_x(i, _):
                    r = pl.ds(pl.multiple_of(i * 64, 64), 64)
                    xh[r, kspan(k)], xl[r, kspan(k)] = split(xv[r, kspan(k)])
                    return 0

                lax.fori_loop(0, ROWS // 64, split_x, 0)
            load_f[h][k].wait()

            def split_f(i, _):
                r = pl.ds(pl.multiple_of(k * DEPTH + i * 128, 128), 128)
                fh[h, r, :], fl[h, r, :] = split(fv[h, r, :])
                return 0

            lax.fori_loop(0, DEPTH // 128, split_f, 0)
            part = dot3(xh[:, kspan(k)], xl[:, kspan(k)], fh[h, kspan(k), :], fl[h, kspan(k), :])
            p[h] = part if k == 0 else p[h] + part

    project(0)
    pl.semaphore_wait(barrier, len(everyone))
    proj_copy = [start(p.at[0], pr.at[0], partner)]
    x_copy = start(x_hbm.at[:, pl.ds(pl.multiple_of((1 - core) * MINE, MINE), MINE)], xo, other)
    project(1)
    proj_copy.append(start(p.at[1], pr.at[1], partner))

    def turn(src, base, at):
        def body(i, _):
            c = pl.ds(pl.multiple_of(base + i * 128, 128), 128)
            r = pl.ds(pl.multiple_of(i * 128, 128), 128)
            hi, lo = split(src[:, c].T)
            xth[r, at : at + ROWS] = hi
            xtl[r, at : at + ROWS] = lo
            return 0

        lax.fori_loop(0, MINE // 128, body, 0)

    turn(xv, core * MINE, 0)
    x_copy.wait_recv()
    turn(xo, 0, ROWS)

    def squares(h):
        proj_copy[h].wait_recv()
        total = p[h] + pr[h]
        s[h] = total * total
        return start(s.at[h], so.at[h], other)

    contract = (((0,), (0,)), ((), ()))

    def gram(h):
        cols = slice(h * COLS, (h + 1) * COLS)
        g[:, cols] = jnp.zeros((256, COLS), F32)

        def body(k, _):
            r = pl.ds(pl.multiple_of(k * 512, 512), 512)
            g[:, cols] += dot3(fh[core, r, :], fl[core, r, :], fh[h, r, :], fl[h, r, :], contract)
            return 0

        lax.fori_loop(0, HALF // 512, body, 0)

    def stacked(h):
        ah, al = split(s[h])
        bh, bl = split(so[h])
        return jnp.concatenate([ah, bh], axis=0), jnp.concatenate([al, bl], axis=0)

    def moment(h, sh, sl, at, n):
        r = pl.ds(pl.multiple_of(at, n), n)
        mom[h, r, :] = dot3(xth[r, :], xtl[r, :], sh, sl)

    s_copy = squares(0)
    gram(0)
    s_copy.wait_recv()

    y_copy = {}
    sh, sl = stacked(0)

    def y_send(j, q):
        y_copy[(j, q)] = start(
            mom.at[0, pl.ds(pl.multiple_of(y_of(j) * 256, 256), 256), pl.ds(q * 128, 128)],
            yrecv.at[q, j - 1], y_peer(j),
        )

    for j in (2, 1, 3):
        moment(0, sh, sl, y_of(j) * 256, 256)
        y_send(j, 0)
    for j in (2, 1, 3):
        y_send(j, 1)
    moment(0, sh, sl, y * 256, 256)

    s_copy = squares(1)
    gram(1)
    g_copy = start(g, gr, partner)
    s_copy.wait_recv()
    sh, sl = stacked(1)

    def zrows(zz, half):
        return pl.ds(pl.multiple_of(zz * 128 + half * 64, 64), 64)

    ring_copy = {}

    def ring_hop(i, k):
        way, half, hops = STREAMS[i]
        if k > hops:
            return
        r = zrows(z_of(way * (hops + 1 - k)), half)
        if k > 1:
            ring_copy[(i, k - 1)].wait_recv()
            mom[1, r, :] += ring[SLOT[(i, k - 1)]]
        ring_copy[(i, k)] = start(mom.at[1, r, :], ring.at[SLOT[(i, k)]], z_peer(way))

    def ring_step(k):
        for i in range(4):
            ring_hop(i, k)

    moment(1, sh, sl, z_of(4) * 128, 128)
    ring_hop(0, 1)
    ring_hop(1, 1)
    moment(1, sh, sl, z_of(3) * 128, 128)
    ring_hop(2, 1)
    moment(1, sh, sl, z_of(-3) * 128, 128)
    ring_hop(3, 1)
    for j in (2, -2, 1, -1, 0):
        moment(1, sh, sl, z_of(j) * 128, 128)

    ring_step(2)

    g_copy.wait_recv()
    whole = (g[...] + gr[...]) * (1.0 / D)
    g2[core] = whole * whole
    g2_copy = start(g2.at[core], g2.at[core], other)

    xb_copy = {}
    zb_copy = {}

    def y_sum(q):
        for j in (1, 3, 2):
            y_copy[(j, q)].wait_recv()
        mine = mom[0, pl.ds(pl.multiple_of(y * 256, 256), 256), pl.ds(q * 128, 128)]
        acc_b[q] = (mine + yrecv[q, 0]) + (yrecv[q, 1] + yrecv[q, 2])
        xb_copy[q] = start(acc_b.at[q, pl.ds(pl.multiple_of((1 - xhi) * 128, 128), 128), :], xrecv.at[q], yx_peer(1))

    def x_sum(q):
        xb_copy[q].wait_recv()
        acc_b2[q] = acc_b[q, pl.ds(pl.multiple_of(xhi * 128, 128), 128), :] + xrecv[q]
        for j in (4, 3, 5, 2, 6, 1, 7):
            zb_copy[(j, q)] = start(acc_b2.at[q, span(z_of(j) * 16, 16), :], zrecv.at[q, j - 1], z_peer(j))

    y_sum(0)
    ring_step(3)
    row = (y * 256 + xhi * 128 + z * 16, z * 128 + y * 32 + xhi * 16)
    g2_copy.wait_recv()
    for h in range(2):
        part = jnp.zeros((16, COLS), F32)
        for q in range(2):
            ah, al = split(fv[q, span(core * MINE + row[h], 16), :] * (1.0 / 64.0))
            bh, bl = split(g2[q, :, h * COLS : (h + 1) * COLS])
            part += dot3(ah, al, bh, bl)
        term[h] = part
    x_sum(0)
    y_sum(1)
    ring_step(4)
    x_sum(1)

    for half in range(2):
        parts = []
        for i, (way, h, hops) in enumerate(STREAMS):
            if h == half:
                ring_copy[(i, hops)].wait_recv()
                parts.append(ring[SLOT[(i, hops)]])
        acc_a[half * 64 : half * 64 + 64, :] = mom[1, zrows(z, half), :] + (parts[0] + parts[1])
    da_copy = {}
    for j in (5, 4, 1, 3, 7, 2, 6):
        a, b = yx_of(j)
        da_copy[j] = start(acc_a.at[span(a * 32 + b * 16, 16), :], dir_a.at[j - 1], yx_peer(j))

    def finish(h, total):
        return (6.0 / 64.0) * (term[h] - total * (1.0 / (NROWS * D)))

    base = core * MINE
    forward = []
    waiting = []
    rate = []

    def update(h, at, n):
        r = span(at, n)
        o_ref[r, h * COLS : (h + 1) * COLS] = fv[h, r, :] - grad[h, r, :] * rate[0]

    def arrived(h, at, n):
        r = span(base + at, n)
        c = start(grad.at[h, r, :], grad.at[h, r, :], other)
        forward.append((c, h, at, n))
        if rate:
            update(h, base + at, n)
        else:
            waiting.append((h, at, n))

    owns = []
    for q in range(2):
        part = acc_b2[q, span(z * 16, 16), :]
        for j in range(1, 8):
            zb_copy[(j, q)].wait_recv()
        for j in range(1, 8):
            part = part + zrecv[q, j - 1]
        owns.append(part)
    gb = finish(0, jnp.concatenate(owns, axis=1))
    mine_b = span(base + row[0], 16)
    grad[0, mine_b, :] = gb
    zg_copy = [start(grad.at[0, mine_b, :], grad.at[0, mine_b, :], z_peer(j)) for j in (4, 3, 5, 2, 6, 1, 7)]

    own = acc_a[span(y * 32 + xhi * 16, 16), :]
    for j in range(1, 8):
        da_copy[j].wait_recv()
    for j in range(1, 8):
        own = own + dir_a[j - 1]
    ga = finish(1, own)
    mine_a = span(base + row[1], 16)
    grad[1, mine_a, :] = ga
    aa_copy = [start(grad.at[1, mine_a, :], grad.at[1, mine_a, :], yx_peer(j)) for j in (5, 4, 1, 3, 7, 2, 6)]

    sq = ga * ga + gb * gb
    tile = (sq[0:8, 0:128] + sq[8:16, 0:128]) + (sq[0:8, 128:256] + sq[8:16, 128:256])
    me1 = y * 2 + xhi
    ss1[me1] = tile
    s1_copy = [start(ss1.at[me1], ss1.at[me1], yx_peer(j)) for j in range(1, 8)]

    for c in zg_copy:
        c.wait_recv()
    yg_copy = {}

    def y_spread(i):
        at = y * 256 + (xhi * 128 if i == 0 else (1 - xhi) * 128)
        r = span(base + at, 128)
        for q in (2, 1, 3):
            yg_copy[(i, q)] = start(grad.at[0, r, :], grad.at[0, r, :], y_peer(q))
        arrived(0, at, 128)

    r = span(base + y * 256 + xhi * 128, 128)
    xg_copy = start(grad.at[0, r, :], grad.at[0, r, :], yx_peer(1))
    y_spread(0)

    for c in aa_copy:
        c.wait_recv()
    gather = {}

    def gather_step(k):
        for i, (way, half, hops) in enumerate(STREAMS):
            if k > hops + 1:
                continue
            at = z_of(-way * (k - 1)) * 128 + half * 64
            r = span(base + at, 64)
            if k > 1:
                gather[(i, k - 1)].wait_recv()
            if k <= hops:
                gather[(i, k)] = start(grad.at[1, r, :], grad.at[1, r, :], z_peer(way))
            if k > 1:
                arrived(1, at, 64)

    gather_step(1)
    arrived(1, z * 128, 128)
    for c in s1_copy:
        c.wait_recv()
    tile = ss1[0]
    for j in range(1, 8):
        tile = tile + ss1[j]
    ss2[z] = tile
    s2_copy = [start(ss2.at[z], ss2.at[z], z_peer(j)) for j in range(1, 8)]
    xg_copy.wait_recv()
    y_spread(1)
    gather_step(2)
    for c in s2_copy:
        c.wait_recv()
    tile = ss2[0]
    for j in range(1, 8):
        tile = tile + ss2[j]
    ss3[core] = tile
    s3_copy = start(ss3.at[core], ss3.at[core], other)
    gather_step(3)
    s3_copy.wait_recv()
    ss4[feat] = ss3[0] + ss3[1]
    s4_copy = start(ss4.at[feat], ss4.at[feat], partner)
    gather_step(4)
    s4_copy.wait_recv()
    total = jnp.sum(ss4[0] + ss4[1], keepdims=True)
    rms = jnp.sqrt(total * (1.0 / (D * R))) + 1e-06
    rate.append(0.5 / rms)
    for h, at, n in waiting:
        update(h, base + at, n)
    over = (1 - core) * MINE

    def from_other(upto):
        while len(done) < upto:
            c, h, at, n = forward[len(done)]
            c.wait_recv()
            update(h, over + at, n)
            done.append(0)

    done = []
    from_other(len(forward))

    def y_land(i):
        for q in (1, 3, 2):
            yg_copy[(i, q)].wait_recv()
            arrived(0, y_of(-q) * 256 + (xhi * 128 if i == 0 else (1 - xhi) * 128), 128)

    y_land(0)
    gather_step(5)
    from_other(len(forward) - 4)
    y_land(1)
    from_other(len(forward))
    for c in unsent:
        c.wait_send()


NSEM = 224


def per_device(samples, factor):
    vm = pltpu.VMEM
    scratch = [
        vm((ROWS, HALF), F32), vm((ROWS, MINE), F32), vm((2, HALF, COLS), F32),
        vm((2, HALF, COLS), BF16), vm((2, HALF, COLS), BF16),
        vm((ROWS, HALF), BF16), vm((ROWS, HALF), BF16),
        vm((2, ROWS, COLS), F32), vm((2, ROWS, COLS), F32), vm((2, ROWS, COLS), F32), vm((2, ROWS, COLS), F32),
        vm((MINE, 2 * ROWS), BF16), vm((MINE, 2 * ROWS), BF16), vm((2, MINE, COLS), F32),
        vm((NSLOT, 64, COLS), F32), vm((128, COLS), F32), vm((7, 16, COLS), F32),
        vm((2, 3, 256, 128), F32), vm((2, 256, 128), F32), vm((2, 7, 16, 128), F32),
        vm((2, 128, 128), F32), vm((2, 128, 128), F32),
        vm((256, R), F32), vm((256, R), F32), vm((2, 256, R), F32), vm((2, 16, COLS), F32),
        vm((2, HALF, COLS), F32),
        vm((8, 8, 128), F32), vm((8, 8, 128), F32), vm((2, 8, 128), F32), vm((2, 8, 128), F32),
        pltpu.SemaphoreType.DMA((12,)), pltpu.SemaphoreType.DMA((NSEM,)), pltpu.SemaphoreType.DMA((NSEM,)),
    ]
    return pl.pallas_call(
        kernel,
        out_shape=pltpu.VMEM((HALF, R), F32),
        in_specs=[pl.BlockSpec(memory_space=pltpu.HBM)] * 2,
        out_specs=pl.BlockSpec(memory_space=pltpu.VMEM),
        scratch_shapes=scratch,
        name="cp_step",
        cost_estimate=pl.CostEstimate(flops=10**10, bytes_accessed=10**7, transcendentals=0),
        compiler_params=pltpu.CompilerParams(
            collective_id=0, has_side_effects=True, vmem_limit_bytes=50 * 2**20
        ),
    )(samples, factor)


def solution(mesh):
    placed = (P("samples", "feat"), P("feat", None))
    return jax.shard_map(
        per_device, mesh=mesh, in_specs=placed, out_specs=P("feat", None), check_vma=False
    )
```

time: 91.7 us -> 80.8 us (0.88)
  Pallas kernels: 85.3 us -> 78.7 us
  local copies, waits for them, and re-layouts: 6.23 us -> 2.02 us
    pallas_call x1, Pallas kernels: 85.3 us -> 78.7 us  [per_device(): pl.pallas_call(kernel, out_shape=pltpu.VMEM((HALF, R), F32), in_specs=[pl...]
    unnamed x3 -> x1, local copies, waits for them, and re-layouts: 6.23 us -> 2.02 us
where the time goes in v2:
time: 80.8 us
  Pallas kernels  78.7 us (97%)
  local copies, waits for them, and re-layouts  2.02 us (2%)
    pallas_call x1, Pallas kernels, per_device(): pl.pallas_call(kernel, out_shape=pltpu.VMEM((HALF, R), F32), in_specs=[pl...  78.7 us
    unnamed x1, local copies, waits for them, and re-layouts  2.02 us

profile of v2, /device:TPU:1, one launch (start us, length us, event | category | flops | bytes accessed | tf_op | source)
XLA Modules:
  0.0 80.8 jit_solution(6479227938313384385)
XLA Ops:
  0.0 78.7 %cp_step.1 = f32[2048,512]{1,0:T(8,128)S(1)} custom-call(f32[256,2048]{1,0:T(8,128)} %x_hbm.1, f32[2048,512]{1,0:T(8,128)} %f_hbm.1), custom_call_target="tpu_custom_call" | custom-call | flops 10000000000 | bytes 10000000 | tf_op jit(solution)/shard_map/cp_step/pallas_call | solution.py:455
  78.8 2.0 %copy.4 = f32[2048,512]{1,0:T(8,128)} copy(f32[2048,512]{1,0:T(8,128)S(1)} %cp_step.1) | data formatting | bytes 8388608

commit v3 on v2

v3 whole, which is shorter than its diff:
```python
import jax
import jax.numpy as jnp
from jax import lax
from jax.experimental import pallas as pl
from jax.experimental.pallas import tpu as pltpu
from jax.sharding import PartitionSpec as P

D = 4096
R = 512
NROWS = 32768
HALF = D // 2
ROWS = 256
COLS = 256
DEPTH = 512
MINE = HALF // 2
MESH = pl.DeviceIdType.MESH
F32 = jnp.float32
BF16 = jnp.bfloat16

STREAMS = ((1, 0, 4), (-1, 1, 4), (1, 1, 3), (-1, 0, 3))
SLOT = {}
for _k in range(1, 5):
    for _i, (_, _, _hops) in enumerate(STREAMS):
        if _k <= _hops:
            SLOT[(_i, _k)] = len(SLOT)
NSLOT = len(SLOT)


def split(v):
    hi = v.astype(BF16)
    return hi, (v - hi.astype(F32)).astype(BF16)


def dot3(ah, al, bh, bl, dims=(((1,), (0,)), ((), ()))):
    def one(a, b):
        return lax.dot_general(a, b, dims, preferred_element_type=F32)

    return one(ah, bh) + (one(ah, bl) + one(al, bh))


def kernel(
    x_hbm, f_hbm, o_ref,
    xv, xo, fv, fh, fl, xh, xl, p, pr, s, so, xth, xtl, mom,
    ring, acc_a, dir_a, yrecv, acc_b, zrecv, acc_b2, xrecv,
    gram, gram_mine, gram_other, wh, wl, grad, ss1, ss2, ss3, ss4,
    load_sem, send, recv,
):
    sidx = lax.axis_index("samples")
    feat = lax.axis_index("feat")
    core = lax.rem(sidx, 2)
    z = lax.rem(sidx // 2, 8)
    y = lax.rem(sidx // 16, 4)
    xhi = sidx // 64

    def dev(a, b, c, d, e):
        return (((a * 4 + b) * 8 + c) * 2 + d, e)

    other = dev(xhi, y, z, 1 - core, feat)
    partner = dev(xhi, y, z, core, 1 - feat)

    def yx_of(j):
        return lax.rem(y + j // 2, 4), lax.rem(xhi + j % 2, 2)

    def yx_peer(j):
        a, b = yx_of(j)
        return dev(b, a, z, core, feat)

    def y_of(j):
        return lax.rem(y + j + 4, 4)

    def y_peer(j):
        return dev(xhi, y_of(j), z, core, feat)

    def z_of(j):
        return lax.rem(z + j + 8, 8)

    def z_peer(j):
        return dev(xhi, y, z_of(j), core, feat)

    def span(at, n):
        return pl.ds(pl.multiple_of(at, 16), n)

    counter = [0]
    unsent = []

    def start(src, dst, to):
        i = counter[0]
        counter[0] += 1
        c = pltpu.make_async_remote_copy(
            src_ref=src, dst_ref=dst, send_sem=send.at[i], recv_sem=recv.at[i],
            device_id=to, device_id_type=MESH,
        )
        c.start()
        unsent.append(c)
        return c

    def kspan(k):
        return pl.ds(k * DEPTH, DEPTH)

    load_x = [pltpu.make_async_copy(x_hbm.at[:, kspan(k)], xv.at[:, kspan(k)], load_sem.at[k]) for k in range(4)]
    load_f = [
        [
            pltpu.make_async_copy(
                f_hbm.at[kspan(k), pl.ds(h * COLS, COLS)], fv.at[h, kspan(k), :], load_sem.at[4 + 4 * h + k]
            )
            for k in range(4)
        ]
        for h in range(2)
    ]
    for k in range(4):
        load_x[k].start()
        load_f[0][k].start()
    for k in range(4):
        load_f[1][k].start()
    barrier = pltpu.get_barrier_semaphore()
    everyone = [other, partner] + [yx_peer(j) for j in range(1, 8)] + [z_peer(j) for j in range(1, 8)]
    for to in everyone:
        pl.semaphore_signal(barrier, inc=1, device_id=to, device_id_type=MESH)

    def split_factor(h, k):
        load_f[h][k].wait()

        def body(i, _):
            r = pl.ds(pl.multiple_of(k * DEPTH + i * 128, 128), 128)
            fh[h, r, :], fl[h, r, :] = split(fv[h, r, :])
            return 0

        lax.fori_loop(0, DEPTH // 128, body, 0)

    def project(h):
        for k in range(4):
            if h == 0:
                load_x[k].wait()

                def split_x(i, _):
                    r = pl.ds(pl.multiple_of(i * 64, 64), 64)
                    xh[r, kspan(k)], xl[r, kspan(k)] = split(xv[r, kspan(k)])
                    return 0

                lax.fori_loop(0, ROWS // 64, split_x, 0)
            if h == 0:
                split_factor(0, k)
            part = dot3(xh[:, kspan(k)], xl[:, kspan(k)], fh[h, kspan(k), :], fl[h, kspan(k), :])
            for i in range(2):
                piece = part[:, i * 128 : (i + 1) * 128]
                p[2 * h + i] = piece if k == 0 else p[2 * h + i] + piece

    proj_copy = {}

    def exchange(h):
        for q in (2 * h, 2 * h + 1):
            proj_copy[q] = start(p.at[q], pr.at[q], partner)

    project(0)
    pl.semaphore_wait(barrier, len(everyone))
    exchange(0)
    x_copy = start(x_hbm.at[:, pl.ds(pl.multiple_of((1 - core) * MINE, MINE), MINE)], xo, other)
    for k in range(4):
        split_factor(1, k)

    contract = (((0,), (0,)), ((), ()))
    chip = (xhi * 4 + y) * 8 + z
    block = chip // 16
    block_at = pl.ds(pl.multiple_of(lax.rem(block, 2) * 128, 128), 128)
    block_half = block // 2
    eight = pl.ds(pl.multiple_of(lax.rem(chip, 16) * 8, 8), 8)
    for h in range(2):
        cols = slice(h * COLS, (h + 1) * COLS)
        for k in range(4):
            part = dot3(
                fh[block_half, kspan(k), block_at], fl[block_half, kspan(k), block_at],
                fh[h, kspan(k), :], fl[h, kspan(k), :], contract,
            )
            gram[:, cols] = part if k == 0 else gram[:, cols] + part
    gram_mine[...] = gram[eight, :]
    g_copy = start(gram_mine, gram_other, partner)

    project(1)
    exchange(1)

    def turn(src, base, at):
        def body(i, _):
            c = pl.ds(pl.multiple_of(base + i * 128, 128), 128)
            r = pl.ds(pl.multiple_of(i * 128, 128), 128)
            hi, lo = split(src[:, c].T)
            xth[r, at : at + ROWS] = hi
            xtl[r, at : at + ROWS] = lo
            return 0

        lax.fori_loop(0, MINE // 128, body, 0)

    turn(xv, core * MINE, 0)
    x_copy.wait_recv()
    turn(xo, 0, ROWS)

    base = core * MINE
    s_copy = {}

    def squares(q):
        proj_copy[q].wait_recv()
        total = p[q] + pr[q]
        s[q] = total * total
        s_copy[q] = start(s.at[q], so.at[q], other)

    def stacked(q):
        s_copy[q].wait_recv()
        ah, al = split(s[q])
        bh, bl = split(so[q])
        return jnp.concatenate([ah, bh], axis=0), jnp.concatenate([al, bl], axis=0)

    def moment(q, sh, sl, at, n):
        r = pl.ds(pl.multiple_of(at, n), n)
        w = pl.ds(pl.multiple_of(base + at, n), n)
        cols = slice(q * 128, (q + 1) * 128)
        mom[q, r, :] = dot3(xth[r, :], xtl[r, :], sh, sl) - dot3(
            fh[block_half, w, block_at], fl[block_half, w, block_at], wh[:, cols], wl[:, cols]
        )

    y_copy, xb_copy, zb_copy = {}, {}, {}

    def y_start(q):
        sh, sl = stacked(q)
        for j in (2, 1, 3):
            moment(q, sh, sl, y_of(j) * 256, 256)
            y_copy[(j, q)] = start(
                mom.at[q, pl.ds(pl.multiple_of(y_of(j) * 256, 256), 256), :], yrecv.at[q // 2, j - 1], y_peer(j)
            )
        moment(q, sh, sl, y * 256, 256)

    def y_sum(q):
        for j in (1, 3, 2):
            y_copy[(j, q)].wait_recv()
        i = q // 2
        mine = mom[q, pl.ds(pl.multiple_of(y * 256, 256), 256), :]
        acc_b[i] = (mine + yrecv[i, 0]) + (yrecv[i, 1] + yrecv[i, 2])
        xb_copy[q] = start(acc_b.at[i, pl.ds(pl.multiple_of((1 - xhi) * 128, 128), 128), :], xrecv.at[i], yx_peer(1))

    def x_sum(q):
        i = q // 2
        xb_copy[q].wait_recv()
        acc_b2[i] = acc_b[i, pl.ds(pl.multiple_of(xhi * 128, 128), 128), :] + xrecv[i]
        for j in (4, 3, 5, 2, 6, 1, 7):
            zb_copy[(j, q)] = start(acc_b2.at[i, span(z_of(j) * 16, 16), :], zrecv.at[i, j - 1], z_peer(j))

    def z_sum(q):
        i = q // 2
        part = acc_b2[i, span(z * 16, 16), :]
        for j in range(1, 8):
            zb_copy[(j, q)].wait_recv()
        for j in range(1, 8):
            part = part + zrecv[i, j - 1]
        return part

    def zrows(zz, half):
        return pl.ds(pl.multiple_of(zz * 128 + half * 64, 64), 64)

    ring_copy, da_copy = {}, {}

    def ring_hop(q, i, k):
        way, half, hops = STREAMS[i]
        if k > hops:
            return
        r = zrows(z_of(way * (hops + 1 - k)), half)
        if k > 1:
            ring_copy[(q, i, k - 1)].wait_recv()
            mom[q, r, :] += ring[q // 2, SLOT[(i, k - 1)]]
        ring_copy[(q, i, k)] = start(mom.at[q, r, :], ring.at[q // 2, SLOT[(i, k)]], z_peer(way))

    def ring_step(q, k):
        for i in range(4):
            ring_hop(q, i, k)

    def ring_start(q):
        sh, sl = stacked(q)
        moment(q, sh, sl, z_of(4) * 128, 128)
        ring_hop(q, 0, 1)
        ring_hop(q, 1, 1)
        moment(q, sh, sl, z_of(3) * 128, 128)
        ring_hop(q, 2, 1)
        moment(q, sh, sl, z_of(-3) * 128, 128)
        ring_hop(q, 3, 1)
        for j in (2, -2, 1, -1, 0):
            moment(q, sh, sl, z_of(j) * 128, 128)

    def ring_end(q):
        for half in range(2):
            parts = []
            for i, (way, h, hops) in enumerate(STREAMS):
                if h == half:
                    ring_copy[(q, i, hops)].wait_recv()
                    parts.append(ring[q // 2, SLOT[(i, hops)]])
            acc_a[q // 2, half * 64 : half * 64 + 64, :] = mom[q, zrows(z, half), :] + (parts[0] + parts[1])
        for j in (5, 4, 1, 3, 7, 2, 6):
            a, b = yx_of(j)
            da_copy[(j, q)] = start(acc_a.at[q // 2, span(a * 32 + b * 16, 16), :], dir_a.at[q // 2, j - 1], yx_peer(j))

    def direct_sum(q):
        part = acc_a[q // 2, span(y * 32 + xhi * 16, 16), :]
        for j in range(1, 8):
            da_copy[(j, q)].wait_recv()
        for j in range(1, 8):
            part = part + dir_a[q // 2, j - 1]
        return part

    def gram_weights():
        gram[...] = jnp.zeros_like(gram)
        g_copy.wait_recv()
        whole = (gram_mine[...] + gram_other[...]) * (1.0 / D)
        gram[eight, :] = whole * whole * (NROWS * D / 64.0)
        wh[...], wl[...] = split(gram[...])

    row = (y * 256 + xhi * 128 + z * 16, z * 128 + y * 32 + xhi * 16)

    squares_of = []

    def finish(q, total):
        gq = total * (-6.0 / 64.0 / (NROWS * D))
        squares_of.append(gq * gq)
        grad[q, span(base + row[q % 2], 16), :] = gq

    forward = []
    waiting = []
    rate = []
    zg_copy, xg_copy, yg_copy, aa_copy, gather = {}, {}, {}, {}, {}

    def update(q, at, n):
        r = span(at, n)
        c = (q % 2) * 128
        o_ref[r, q * 128 : (q + 1) * 128] = fv[q // 2, r, c : c + 128] - grad[q, r, :] * rate[0]

    def send_rows(q, at, n, to):
        r = span(base + at, n)
        return start(grad.at[q, r, :], grad.at[q, r, :], to)

    def arrived(q, at, n):
        forward.append((send_rows(q, at, n, other), q, at, n))
        if rate:
            update(q, base + at, n)
        else:
            waiting.append((q, at, n))

    def own_y(q):
        finish(q, z_sum(q))
        zg_copy[q] = [send_rows(q, row[0], 16, z_peer(j)) for j in (4, 3, 5, 2, 6, 1, 7)]

    def own_ring(q):
        finish(q, direct_sum(q))
        aa_copy[q] = [send_rows(q, row[1], 16, yx_peer(j)) for j in (5, 4, 1, 3, 7, 2, 6)]

    def y_rows(yy, i):
        return yy * 256 + (xhi * 128 if i == 0 else (1 - xhi) * 128)

    def y_spread(q, i):
        at = y_rows(y, i)
        if i == 0:
            for c in zg_copy[q]:
                c.wait_recv()
            xg_copy[q] = send_rows(q, at, 128, yx_peer(1))
        else:
            xg_copy[q].wait_recv()
        for j in (2, 1, 3):
            yg_copy[(q, i, j)] = send_rows(q, at, 128, y_peer(j))
        arrived(q, at, 128)

    def y_land(q, i):
        for j in (1, 3, 2):
            yg_copy[(q, i, j)].wait_recv()
            arrived(q, y_rows(y_of(-j), i), 128)

    def gather_step(q, k):
        if k == 1:
            for c in aa_copy[q]:
                c.wait_recv()
        for i, (way, half, hops) in enumerate(STREAMS):
            if k > hops + 1:
                continue
            at = z_of(-way * (k - 1)) * 128 + half * 64
            if k > 1:
                gather[(q, i, k - 1)].wait_recv()
            if k <= hops:
                gather[(q, i, k)] = send_rows(q, at, 64, z_peer(way))
            if k > 1:
                arrived(q, at, 64)
        if k == 1:
            arrived(q, z * 128, 128)

    done = []

    def from_other(upto):
        while len(done) < upto:
            c, q, at, n = forward[len(done)]
            c.wait_recv()
            update(q, (1 - core) * MINE + at, n)
            done.append(0)

    squares(0)
    gram_weights()
    y_start(0)
    squares(1)
    ring_start(1)
    squares(2)
    y_start(2)
    squares(3)
    ring_step(1, 2)
    ring_start(3)
    ring_step(1, 3)
    y_sum(0)
    ring_step(3, 2)
    ring_step(1, 4)
    x_sum(0)
    ring_step(3, 3)
    y_sum(2)
    ring_end(1)
    own_y(0)
    ring_step(3, 4)
    x_sum(2)
    own_ring(1)
    ring_end(3)
    y_spread(0, 0)
    own_y(2)
    gather_step(1, 1)
    own_ring(3)
    sq = (squares_of[0] + squares_of[1]) + (squares_of[2] + squares_of[3])
    me1 = y * 2 + xhi
    ss1[me1] = sq[0:8] + sq[8:16]
    s1_copy = [start(ss1.at[me1], ss1.at[me1], yx_peer(j)) for j in range(1, 8)]
    y_spread(0, 1)
    y_spread(2, 0)
    gather_step(1, 2)
    for c in s1_copy:
        c.wait_recv()
    tile = ss1[0]
    for j in range(1, 8):
        tile = tile + ss1[j]
    ss2[z] = tile
    s2_copy = [start(ss2.at[z], ss2.at[z], z_peer(j)) for j in range(1, 8)]
    gather_step(3, 1)
    gather_step(1, 3)
    y_spread(2, 1)
    gather_step(3, 2)
    gather_step(1, 4)
    for c in s2_copy:
        c.wait_recv()
    tile = ss2[0]
    for j in range(1, 8):
        tile = tile + ss2[j]
    ss3[core] = tile
    s3_copy = start(ss3.at[core], ss3.at[core], other)
    y_land(0, 0)
    s3_copy.wait_recv()
    ss4[feat] = ss3[0] + ss3[1]
    s4_copy = start(ss4.at[feat], ss4.at[feat], partner)
    y_land(0, 1)
    gather_step(3, 3)
    gather_step(1, 5)
    s4_copy.wait_recv()
    total = jnp.sum(ss4[0] + ss4[1], keepdims=True)
    rms = jnp.sqrt(total * (1.0 / (D * R))) + 1e-06
    rate.append(0.5 / rms)
    for q, at, n in waiting:
        update(q, base + at, n)
    gather_step(3, 4)
    y_land(2, 0)
    from_other(len(forward) - 8)
    y_land(2, 1)
    gather_step(3, 5)
    from_other(len(forward))
    for c in unsent:
        c.wait_send()


NSEM = 256


def per_device(samples, factor):
    vm = pltpu.VMEM
    scratch = [
        vm((ROWS, HALF), F32), vm((ROWS, MINE), F32), vm((2, HALF, COLS), F32),
        vm((2, HALF, COLS), BF16), vm((2, HALF, COLS), BF16),
        vm((ROWS, HALF), BF16), vm((ROWS, HALF), BF16),
        vm((4, ROWS, 128), F32), vm((4, ROWS, 128), F32), vm((4, ROWS, 128), F32), vm((4, ROWS, 128), F32),
        vm((MINE, 2 * ROWS), BF16), vm((MINE, 2 * ROWS), BF16), vm((4, MINE, 128), F32),
        vm((2, NSLOT, 64, 128), F32), vm((2, 128, 128), F32), vm((2, 7, 16, 128), F32),
        vm((2, 3, 256, 128), F32), vm((2, 256, 128), F32), vm((2, 7, 16, 128), F32),
        vm((2, 128, 128), F32), vm((2, 128, 128), F32),
        vm((128, R), F32), vm((8, R), F32), vm((8, R), F32), vm((128, R), BF16), vm((128, R), BF16),
        vm((4, HALF, 128), F32),
        vm((8, 8, 128), F32), vm((8, 8, 128), F32), vm((2, 8, 128), F32), vm((2, 8, 128), F32),
        pltpu.SemaphoreType.DMA((12,)), pltpu.SemaphoreType.DMA((NSEM,)), pltpu.SemaphoreType.DMA((NSEM,)),
    ]
    return pl.pallas_call(
        kernel,
        out_shape=pltpu.VMEM((HALF, R), F32),
        in_specs=[pl.BlockSpec(memory_space=pltpu.HBM)] * 2,
        out_specs=pl.BlockSpec(memory_space=pltpu.VMEM),
        scratch_shapes=scratch,
        name="cp_step",
        cost_estimate=pl.CostEstimate(flops=10**10, bytes_accessed=10**7, transcendentals=0),
        compiler_params=pltpu.CompilerParams(
            collective_id=0, has_side_effects=True, vmem_limit_bytes=50 * 2**20
        ),
    )(samples, factor)


def solution(mesh):
    placed = (P("samples", "feat"), P("feat", None))
    return jax.shard_map(
        per_device, mesh=mesh, in_specs=placed, out_specs=P("feat", None), check_vma=False
    )
```

time: 80.8 us -> 75.5 us (0.934)
  Pallas kernels: 78.7 us -> 73.4 us
    pallas_call x1, Pallas kernels: 78.7 us -> 73.4 us  [per_device(): pl.pallas_call(kernel, out_shape=pltpu.VMEM((HALF, R), F32), in_specs=[pl...]
where the time goes in v3:
time: 75.5 us; the launch traced here: 75.4 us
  Pallas kernels  73.4 us (97%)
  local copies, waits for them, and re-layouts  2.02 us (3%)
    pallas_call x1, Pallas kernels, per_device(): pl.pallas_call(kernel, out_shape=pltpu.VMEM((HALF, R), F32), in_specs=[pl...  73.4 us
    unnamed x1, local copies, waits for them, and re-layouts  2.02 us

profile of v3, /device:TPU:1, one launch (start us, length us, event | category | flops | bytes accessed | tf_op | source)
XLA Modules:
  0.0 75.4 jit_solution(4550193890121223808)
XLA Ops:
  0.0 73.4 %cp_step.1 = f32[2048,512]{1,0:T(8,128)S(1)} custom-call(f32[256,2048]{1,0:T(8,128)} %x_hbm.1, f32[2048,512]{1,0:T(8,128)} %f_hbm.1), custom_call_target="tpu_custom_call" | custom-call | flops 10000000000 | bytes 10000000 | tf_op jit(solution)/shard_map/cp_step/pallas_call | solution.py:491
  73.4 2.0 %copy.4 = f32[2048,512]{1,0:T(8,128)} copy(f32[2048,512]{1,0:T(8,128)S(1)} %cp_step.1) | data formatting | bytes 8388608

commit v4 on v3

--- a/solution.py
+++ b/solution.py
@@ -316,7 +316,7 @@
     def finish(q, total):
         gq = total * (-6.0 / 64.0 / (NROWS * D))
         squares_of.append(gq * gq)
-        grad[q, span(base + row[q % 2], 16), :] = gq
+        grad[q, span(base + row[1 - q % 2], 16), :] = gq
 
     forward = []
     waiting = []
@@ -395,38 +395,37 @@
 
     squares(0)
     gram_weights()
-    y_start(0)
+    ring_start(0)
     squares(1)
-    ring_start(1)
+    y_start(1)
     squares(2)
-    y_start(2)
+    ring_step(0, 2)
+    ring_start(2)
     squares(3)
-    ring_step(1, 2)
-    ring_start(3)
-    ring_step(1, 3)
-    y_sum(0)
-    ring_step(3, 2)
-    ring_step(1, 4)
-    x_sum(0)
-    ring_step(3, 3)
-    y_sum(2)
-    ring_end(1)
-    own_y(0)
-    ring_step(3, 4)
-    x_sum(2)
-    own_ring(1)
-    ring_end(3)
-    y_spread(0, 0)
-    own_y(2)
-    gather_step(1, 1)
-    own_ring(3)
+    ring_step(0, 3)
+    y_start(3)
+    ring_step(2, 2)
+    ring_step(0, 4)
+    y_sum(1)
+    ring_step(2, 3)
+    ring_end(0)
+    x_sum(1)
+    ring_step(2, 4)
+    y_sum(3)
+    own_ring(0)
+    own_y(1)
+    ring_end(2)
+    x_sum(3)
+    gather_step(0, 1)
+    y_spread(1, 0)
+    own_ring(2)
+    own_y(3)
     sq = (squares_of[0] + squares_of[1]) + (squares_of[2] + squares_of[3])
     me1 = y * 2 + xhi
     ss1[me1] = sq[0:8] + sq[8:16]
     s1_copy = [start(ss1.at[me1], ss1.at[me1], yx_peer(j)) for j in range(1, 8)]
-    y_spread(0, 1)
-    y_spread(2, 0)
-    gather_step(1, 2)
+    y_spread(1, 1)
+    gather_step(0, 2)
     for c in s1_copy:
         c.wait_recv()
     tile = ss1[0]
@@ -434,11 +433,12 @@
         tile = tile + ss1[j]
     ss2[z] = tile
     s2_copy = [start(ss2.at[z], ss2.at[z], z_peer(j)) for j in range(1, 8)]
-    gather_step(3, 1)
-    gather_step(1, 3)
-    y_spread(2, 1)
-    gather_step(3, 2)
-    gather_step(1, 4)
+    gather_step(2, 1)
+    y_spread(3, 0)
+    gather_step(0, 3)
+    y_spread(3, 1)
+    gather_step(2, 2)
+    gather_step(0, 4)
     for c in s2_copy:
         c.wait_recv()
     tile = ss2[0]
@@ -446,24 +446,24 @@
         tile = tile + ss2[j]
     ss3[core] = tile
     s3_copy = start(ss3.at[core], ss3.at[core], other)
-    y_land(0, 0)
+    y_land(1, 0)
     s3_copy.wait_recv()
     ss4[feat] = ss3[0] + ss3[1]
     s4_copy = start(ss4.at[feat], ss4.at[feat], partner)
-    y_land(0, 1)
-    gather_step(3, 3)
-    gather_step(1, 5)
+    y_land(1, 1)
+    gather_step(2, 3)
+    gather_step(0, 5)
     s4_copy.wait_recv()
     total = jnp.sum(ss4[0] + ss4[1], keepdims=True)
     rms = jnp.sqrt(total * (1.0 / (D * R))) + 1e-06
     rate.append(0.5 / rms)
     for q, at, n in waiting:
         update(q, base + at, n)
-    gather_step(3, 4)
-    y_land(2, 0)
+    y_land(3, 0)
+    gather_step(2, 4)
     from_other(len(forward) - 8)
-    y_land(2, 1)
-    gather_step(3, 5)
+    y_land(3, 1)
+    gather_step(2, 5)
     from_other(len(forward))
     for c in unsent:
         c.wait_send()

time: 75.5 us -> 73.3 us (0.971)
  Pallas kernels: 73.4 us -> 71.2 us
    pallas_call x1, Pallas kernels: 73.4 us -> 71.2 us  [per_device(): pl.pallas_call(kernel, out_shape=pltpu.VMEM((HALF, R), F32), in_specs=[pl...]
where the time goes in v4:
time: 73.3 us; the launch traced here: 73.2 us
  Pallas kernels  71.2 us (97%)
  local copies, waits for them, and re-layouts  2.02 us (3%)
    pallas_call x1, Pallas kernels, per_device(): pl.pallas_call(kernel, out_shape=pltpu.VMEM((HALF, R), F32), in_specs=[pl...  71.2 us
    unnamed x1, local copies, waits for them, and re-layouts  2.02 us

profile of v4, /device:TPU:1, one launch (start us, length us, event | category | flops | bytes accessed | tf_op | source)
XLA Modules:
  0.0 73.2 jit_solution(14288852694521678422)
XLA Ops:
  0.0 71.2 %cp_step.1 = f32[2048,512]{1,0:T(8,128)S(1)} custom-call(f32[256,2048]{1,0:T(8,128)} %x_hbm.1, f32[2048,512]{1,0:T(8,128)} %f_hbm.1), custom_call_target="tpu_custom_call" | custom-call | flops 10000000000 | bytes 10000000 | tf_op jit(solution)/shard_map/cp_step/pallas_call | solution.py:491
  71.2 2.0 %copy.4 = f32[2048,512]{1,0:T(8,128)} copy(f32[2048,512]{1,0:T(8,128)S(1)} %cp_step.1) | data formatting | bytes 8388608

commit v5 on v4

--- a/solution.py
+++ b/solution.py
@@ -93,6 +93,11 @@
         c.start()
         unsent.append(c)
         return c
+
+    barrier = pltpu.get_barrier_semaphore()
+    everyone = [other, partner] + [yx_peer(j) for j in range(1, 8)] + [z_peer(j) for j in range(1, 8)]
+    for to in everyone:
+        pl.semaphore_signal(barrier, inc=1, device_id=to, device_id_type=MESH)
 
     def kspan(k):
         return pl.ds(k * DEPTH, DEPTH)
@@ -112,11 +117,6 @@
         load_f[0][k].start()
     for k in range(4):
         load_f[1][k].start()
-    barrier = pltpu.get_barrier_semaphore()
-    everyone = [other, partner] + [yx_peer(j) for j in range(1, 8)] + [z_peer(j) for j in range(1, 8)]
-    for to in everyone:
-        pl.semaphore_signal(barrier, inc=1, device_id=to, device_id_type=MESH)
-
     def split_factor(h, k):
         load_f[h][k].wait()
 
@@ -147,16 +147,15 @@
 
     proj_copy = {}
 
-    def exchange(h):
-        for q in (2 * h, 2 * h + 1):
-            proj_copy[q] = start(p.at[q], pr.at[q], partner)
+    def exchange(q):
+        proj_copy[q] = start(p.at[q], pr.at[q], partner)
 
     project(0)
     pl.semaphore_wait(barrier, len(everyone))
     exchange(0)
-    x_copy = start(x_hbm.at[:, pl.ds(pl.multiple_of((1 - core) * MINE, MINE), MINE)], xo, other)
     for k in range(4):
         split_factor(1, k)
+    exchange(1)
 
     contract = (((0,), (0,)), ((), ()))
     chip = (xhi * 4 + y) * 8 + z
@@ -174,9 +173,10 @@
             gram[:, cols] = part if k == 0 else gram[:, cols] + part
     gram_mine[...] = gram[eight, :]
     g_copy = start(gram_mine, gram_other, partner)
+    x_copy = start(x_hbm.at[:, pl.ds(pl.multiple_of((1 - core) * MINE, MINE), MINE)], xo, other)
 
     project(1)
-    exchange(1)
+    exchange(2)
 
     def turn(src, base, at):
         def body(i, _):
@@ -190,6 +190,7 @@
         lax.fori_loop(0, MINE // 128, body, 0)
 
     turn(xv, core * MINE, 0)
+    exchange(3)
     x_copy.wait_recv()
     turn(xo, 0, ROWS)
 
@@ -446,13 +447,13 @@
         tile = tile + ss2[j]
     ss3[core] = tile
     s3_copy = start(ss3.at[core], ss3.at[core], other)
-    y_land(1, 0)
     s3_copy.wait_recv()
     ss4[feat] = ss3[0] + ss3[1]
     s4_copy = start(ss4.at[feat], ss4.at[feat], partner)
+    gather_step(2, 3)
+    y_land(1, 0)
+    gather_step(0, 5)
     y_land(1, 1)
-    gather_step(2, 3)
-    gather_step(0, 5)
     s4_copy.wait_recv()
     total = jnp.sum(ss4[0] + ss4[1], keepdims=True)
     rms = jnp.sqrt(total * (1.0 / (D * R))) + 1e-06

time: 73.3 us -> 73.4 us (level)
  no operation moved by 1% of the time
where the time goes in v5:
time: 73.4 us; the launch traced here: 73.3 us
  Pallas kernels  71.3 us (97%)
  local copies, waits for them, and re-layouts  2.02 us (3%)
    pallas_call x1, Pallas kernels, per_device(): pl.pallas_call(kernel, out_shape=pltpu.VMEM((HALF, R), F32), in_specs=[pl...  71.3 us
    unnamed x1, local copies, waits for them, and re-layouts  2.02 us

profile of v5, /device:TPU:1, one launch (start us, length us, event | category | flops | bytes accessed | tf_op | source)
XLA Modules:
  0.0 73.3 jit_solution(7434576834599722773)
XLA Ops:
  0.0 71.3 %cp_step.1 = f32[2048,512]{1,0:T(8,128)S(1)} custom-call(f32[256,2048]{1,0:T(8,128)} %x_hbm.1, f32[2048,512]{1,0:T(8,128)} %f_hbm.1), custom_call_target="tpu_custom_call" | custom-call | flops 10000000000 | bytes 10000000 | tf_op jit(solution)/shard_map/cp_step/pallas_call | solution.py:492
  71.3 2.0 %copy.4 = f32[2048,512]{1,0:T(8,128)} copy(f32[2048,512]{1,0:T(8,128)S(1)} %cp_step.1) | data formatting | bytes 8388608
